TPU v7x, 32 devices: a whole 2x2x4 slice. The times are simulated.
32 devices in a mesh: dp: 8 (over y, x, core), tensor: 4 (over z).
Axes of the slice: x: 2, y: 2, z: 4, core: 2. Of those that a mesh axis runs over, the one named last changes fastest.
Arguments:
- encoder_layer_input: bfloat16 [8, 1024, 512], P('dp'), may hold values from -6 to 6
- decoder_layer_input: bfloat16 [8, 1024, 512], P('dp'), may hold values from -6 to 6
- source_pair_index: int32 [8, 1024], P('dp'), may hold values from 0 to 15, never falling along the last dimension, each value on 1 to 128 neighbouring positions
- target_pair_index: int32 [8, 1024], P('dp'), may hold values from 0 to 15, never falling along the last dimension, each value on 1 to 128 neighbouring positions
- masked: int32 [8, 1024], P('dp'), may hold values 0 or 1
- mask_embed: float32 [512], replicated, may hold values from -6 to 6
- enc_qkv: bfloat16 [3, 512, 512], P(None, None, 'tensor'), may hold values from -0.25 to 0.25
- enc_attn_out: bfloat16 [512, 512], P('tensor'), may hold values from -0.75 to 0.75
- enc_ffn_in: bfloat16 [512, 2048], P(None, 'tensor'), may hold values from -0.25 to 0.25
- enc_ffn_out: bfloat16 [2048, 512], P('tensor'), may hold values from -0.1875 to 0.1875
- dec_self_qkv: bfloat16 [3, 512, 512], P(None, None, 'tensor'), may hold values from -0.25 to 0.25
- dec_self_out: bfloat16 [512, 512], P('tensor'), may hold values from -0.75 to 0.75
- dec_cross_qkv: bfloat16 [3, 512, 512], P(None, None, 'tensor'), may hold values from -0.25 to 0.25
- dec_cross_out: bfloat16 [512, 512], P('tensor'), may hold values from -0.75 to 0.75
- dec_ffn_in: bfloat16 [512, 2048], P(None, 'tensor'), may hold values from -0.25 to 0.25
- dec_ffn_out: bfloat16 [2048, 512], P('tensor'), may hold values from -0.1875 to 0.1875
- norm_gain: float32 [5, 512], replicated, may hold values from 0.1 to 1.9
- norm_shift: float32 [5, 512], replicated, may hold values from -1.5 to 1.5
- encoder_output_cotangent: bfloat16 [8, 1024, 512], P('dp'), may hold values from -6 to 6
- decoder_output_cotangent: bfloat16 [8, 1024, 512], P('dp'), may hold values from -6 to 6
Outputs:
- enc_out: bfloat16 [8, 1024, 512], P('dp')
- dec_out: bfloat16 [8, 1024, 512], P('dp')
- enc_in_grad: float32 [8, 1024, 512], P('dp')
- dec_in_grad: float32 [8, 1024, 512], P('dp')
- mask_embed_grad: float32 [512], replicated
- enc_qkv_grad: float32 [3, 512, 512], P(None, None, 'tensor')
- enc_attn_out_grad: float32 [512, 512], P('tensor')
- enc_ffn_in_grad: float32 [512, 2048], P(None, 'tensor')
- enc_ffn_out_grad: float32 [2048, 512], P('tensor')
- dec_self_qkv_grad: float32 [3, 512, 512], P(None, None, 'tensor')
- dec_self_out_grad: float32 [512, 512], P('tensor')
- dec_cross_qkv_grad: float32 [3, 512, 512], P(None, None, 'tensor')
- dec_cross_out_grad: float32 [512, 512], P('tensor')
- dec_ffn_in_grad: float32 [512, 2048], P(None, 'tensor')
- dec_ffn_out_grad: float32 [2048, 512], P('tensor')
- norm_gain_grad: float32 [5, 512], replicated
- norm_shift_grad: float32 [5, 512], replicated
Inputs may be any that keep to these rules, and one draw needn't show every extreme that they name: `source_pair_index`: within each packed row pair ids never fall and each of the 16 ids labels 1 to 128 consecutive tokens, so every pair has source and target tokens in its rows. `target_pair_index`: within each packed row pair ids never fall and each of the 16 ids labels 1 to 128 consecutive tokens.
All inputs are finite; a program needn't handle non-finite values. No bound on the sum of `masked` on one device may be relied on, other than what follows from the above.
Results may differ from a plain program's by a relative error of at most 0.025.
The roundings to bfloat16 on the way count: a program that leaves them out, or rounds other values in their place, can miss the bound.
Values sent between devices are 32-bit elements; how exact they have to be, the bound alone decides.
A program may use at most 192 MiB of HBM per device.

v0:
```python
import jax
import jax.numpy as jnp
from jax import lax
from jax.sharding import PartitionSpec as P

HEAD_DIM = 64


epsilon = 1e-05
floor_score = -1000000000.0


def norm_forward(totals, norm_gain, norm_shift):
    centered = totals - jnp.mean(totals, axis=-1, keepdims=True)
    inverse = lax.rsqrt(jnp.mean(centered * centered, axis=-1, keepdims=True) + epsilon)
    normed = centered * inverse
    return (normed * norm_gain + norm_shift, (normed, inverse))


def norm_backward(grad_out, saved, norm_gain):
    normed, inverse = saved
    grad_normed = grad_out * norm_gain
    first_mean = jnp.mean(grad_normed, axis=-1, keepdims=True)
    second_mean = jnp.mean(grad_normed * normed, axis=-1, keepdims=True)
    grad_totals = inverse * (grad_normed - first_mean - normed * second_mean)
    return (grad_totals, jnp.sum(grad_out * normed, axis=(0, 1)), jnp.sum(grad_out, axis=(0, 1)))


def project(inputs, weight):
    return jnp.einsum("rld,de->rle", inputs, weight, preferred_element_type=jnp.float32)


def weight_grad(inputs, grads):
    return jnp.einsum("rld,rle->de", inputs, grads, preferred_element_type=jnp.float32)


def back_project(grads, weight):
    return jnp.einsum("rle,de->rld", grads, weight, preferred_element_type=jnp.float32)


def split_heads(matrix):
    return matrix.reshape(matrix.shape[0], matrix.shape[1], matrix.shape[2] // HEAD_DIM, HEAD_DIM)


def masked_scores(queries, keys, query_seg, key_seg):
    raw_scores = jnp.einsum(
        "rqhc,rkhc->rhqk",
        split_heads(queries),
        split_heads(keys),
        preferred_element_type=jnp.float32,
    )
    same_pair = (query_seg[:, :, None] == key_seg[:, None, :])[:, None]
    return jnp.where(same_pair, raw_scores * HEAD_DIM ** (-0.5), floor_score)


def smooth_unit(values):
    return jax.nn.gelu(values, approximate=False)


def attend_forward(query_low, key_low, query_seg, key_seg, qkv_weight, out_weight):
    queries = project(query_low, qkv_weight[0]).astype(jnp.bfloat16)
    keys = project(key_low, qkv_weight[1]).astype(jnp.bfloat16)
    values = project(key_low, qkv_weight[2]).astype(jnp.bfloat16)
    scores = masked_scores(queries, keys, query_seg, key_seg)
    highest = jnp.max(scores, axis=-1, keepdims=True)
    raised = jnp.exp(scores - highest)
    totals = jnp.sum(raised, axis=-1, keepdims=True)
    shares = raised / totals
    log_total = highest + jnp.log(totals)
    mixed = jnp.einsum(
        "rhqk,rkhc->rqhc",
        shares.astype(jnp.bfloat16),
        split_heads(values),
        preferred_element_type=jnp.float32,
    )
    mixed = mixed.reshape(queries.shape).astype(jnp.bfloat16)
    return (project(mixed, out_weight), (queries, keys, values, log_total, mixed))


def attend_backward(
    grad_branch, saved, query_low, key_low, query_seg, key_seg, qkv_weight, out_weight
):
    queries, keys, values, log_total, mixed = saved
    grad_low = grad_branch.astype(jnp.bfloat16)
    grad_out_weight = weight_grad(mixed, grad_low)
    grad_mixed = back_project(grad_low, out_weight).astype(jnp.bfloat16)
    shares = jnp.exp(masked_scores(queries, keys, query_seg, key_seg) - log_total)
    grad_heads = split_heads(grad_mixed)
    grad_values = (
        jnp.einsum(
            "rhqk,rqhc->rkhc",
            shares.astype(jnp.bfloat16),
            grad_heads,
            preferred_element_type=jnp.float32,
        )
        .reshape(values.shape)
        .astype(jnp.bfloat16)
    )
    grad_shares = jnp.einsum(
        "rqhc,rkhc->rhqk", grad_heads, split_heads(values), preferred_element_type=jnp.float32
    )
    inner = jnp.sum(shares * grad_shares, axis=-1, keepdims=True)
    grad_raw = (shares * (grad_shares - inner) * HEAD_DIM ** (-0.5)).astype(jnp.bfloat16)
    grad_queries = (
        jnp.einsum(
            "rhqk,rkhc->rqhc", grad_raw, split_heads(keys), preferred_element_type=jnp.float32
        )
        .reshape(queries.shape)
        .astype(jnp.bfloat16)
    )
    grad_keys = (
        jnp.einsum(
            "rhqk,rqhc->rkhc", grad_raw, split_heads(queries), preferred_element_type=jnp.float32
        )
        .reshape(keys.shape)
        .astype(jnp.bfloat16)
    )
    grad_qkv = jnp.stack(
        [
            weight_grad(query_low, grad_queries),
            weight_grad(key_low, grad_keys),
            weight_grad(key_low, grad_values),
        ]
    )
    query_part = back_project(grad_queries, qkv_weight[0])
    key_part = back_project(grad_keys, qkv_weight[1]) + back_project(grad_values, qkv_weight[2])
    return (query_part, key_part, grad_qkv, grad_out_weight)


def feed_forward(inputs_low, weight_in, weight_out):
    before = project(inputs_low, weight_in)
    hidden = smooth_unit(before).astype(jnp.bfloat16)
    return (project(hidden, weight_out), (before, hidden))


def feed_backward(grad_branch, saved, inputs_low, weight_in, weight_out):
    before, hidden = saved
    grad_low = grad_branch.astype(jnp.bfloat16)
    grad_weight_out = weight_grad(hidden, grad_low)
    grad_hidden = back_project(grad_low, weight_out)
    unused, pullback = jax.vjp(smooth_unit, before)
    grad_before = pullback(grad_hidden)[0].astype(jnp.bfloat16)
    return (
        back_project(grad_before, weight_in),
        weight_grad(inputs_low, grad_before),
        grad_weight_out,
    )


def sublayer_total(partial_value):
    return lax.psum(partial_value, "tensor")


def input_total(partial_value):
    return lax.psum(partial_value, "tensor")


def per_device(
    encoder_layer_input,
    decoder_layer_input,
    source_pair_index,
    target_pair_index,
    masked,
    mask_embed,
    enc_qkv,
    enc_attn_out,
    enc_ffn_in,
    enc_ffn_out,
    dec_self_qkv,
    dec_self_out,
    dec_cross_qkv,
    dec_cross_out,
    dec_ffn_in,
    dec_ffn_out,
    norm_gain,
    norm_shift,
    encoder_output_cotangent,
    decoder_output_cotangent,
):
    source = encoder_layer_input.astype(jnp.float32)
    partial_value, enc_attn_saved = attend_forward(
        encoder_layer_input,
        encoder_layer_input,
        source_pair_index,
        source_pair_index,
        enc_qkv,
        enc_attn_out,
    )
    first, norm_zero = norm_forward(
        source + sublayer_total(partial_value), norm_gain[0], norm_shift[0]
    )
    first_low = first.astype(jnp.bfloat16)
    partial_value, enc_ffn_saved = feed_forward(first_low, enc_ffn_in, enc_ffn_out)
    encoded, norm_one = norm_forward(
        first + sublayer_total(partial_value), norm_gain[1], norm_shift[1]
    )
    encoded_low = encoded.astype(jnp.bfloat16)
    is_masked = masked[:, :, None] == 1
    target = jnp.where(
        is_masked, mask_embed[None, None, :], decoder_layer_input.astype(jnp.float32)
    )
    target_low = target.astype(jnp.bfloat16)
    partial_value, self_saved = attend_forward(
        target_low, target_low, target_pair_index, target_pair_index, dec_self_qkv, dec_self_out
    )
    second, norm_two = norm_forward(
        target + sublayer_total(partial_value), norm_gain[2], norm_shift[2]
    )
    second_low = second.astype(jnp.bfloat16)
    partial_value, cross_saved = attend_forward(
        second_low, encoded_low, target_pair_index, source_pair_index, dec_cross_qkv, dec_cross_out
    )
    third, norm_three = norm_forward(
        second + sublayer_total(partial_value), norm_gain[3], norm_shift[3]
    )
    third_low = third.astype(jnp.bfloat16)
    partial_value, dec_ffn_saved = feed_forward(third_low, dec_ffn_in, dec_ffn_out)
    decoded, norm_four = norm_forward(
        third + sublayer_total(partial_value), norm_gain[4], norm_shift[4]
    )
    grad_sum_four, gain_four, shift_four = norm_backward(
        decoder_output_cotangent.astype(jnp.float32), norm_four, norm_gain[4]
    )
    input_part, grad_dec_ffn_in, grad_dec_ffn_out = feed_backward(
        grad_sum_four, dec_ffn_saved, third_low, dec_ffn_in, dec_ffn_out
    )
    grad_third = grad_sum_four + input_total(input_part)
    grad_sum_three, gain_three, shift_three = norm_backward(grad_third, norm_three, norm_gain[3])
    query_part, key_part, grad_cross_qkv, grad_cross_out = attend_backward(
        grad_sum_three,
        cross_saved,
        second_low,
        encoded_low,
        target_pair_index,
        source_pair_index,
        dec_cross_qkv,
        dec_cross_out,
    )
    query_total, key_total = lax.psum((query_part, key_part), "tensor")
    grad_second = grad_sum_three + query_total
    grad_sum_two, gain_two, shift_two = norm_backward(grad_second, norm_two, norm_gain[2])
    query_part, key_part, grad_self_qkv, grad_self_out = attend_backward(
        grad_sum_two,
        self_saved,
        target_low,
        target_low,
        target_pair_index,
        target_pair_index,
        dec_self_qkv,
        dec_self_out,
    )
    grad_target = grad_sum_two + input_total(query_part + key_part)
    grad_dec_in = jnp.where(is_masked, 0.0, grad_target)
    grad_mask_embed = jnp.sum(jnp.where(is_masked, grad_target, 0.0), axis=(0, 1))
    dec_gain_grad = jnp.stack([gain_two, gain_three, gain_four])
    dec_shift_grad = jnp.stack([shift_two, shift_three, shift_four])
    grad_encoded = encoder_output_cotangent.astype(jnp.float32) + key_total
    grad_sum_one, gain_one, shift_one = norm_backward(grad_encoded, norm_one, norm_gain[1])
    input_part, grad_enc_ffn_in, grad_enc_ffn_out = feed_backward(
        grad_sum_one, enc_ffn_saved, first_low, enc_ffn_in, enc_ffn_out
    )
    grad_first = grad_sum_one + input_total(input_part)
    grad_sum_zero, gain_zero, shift_zero = norm_backward(grad_first, norm_zero, norm_gain[0])
    query_part, key_part, grad_enc_qkv, grad_enc_attn_out = attend_backward(
        grad_sum_zero,
        enc_attn_saved,
        encoder_layer_input,
        encoder_layer_input,
        source_pair_index,
        source_pair_index,
        enc_qkv,
        enc_attn_out,
    )
    grad_enc_in = grad_sum_zero + input_total(query_part + key_part)
    enc_gain_grad = jnp.stack([gain_zero, gain_one])
    enc_shift_grad = jnp.stack([shift_zero, shift_one])
    (
        grad_mask_embed,
        grad_self_qkv,
        grad_self_out,
        grad_cross_qkv,
        grad_cross_out,
        grad_dec_ffn_in,
        grad_dec_ffn_out,
        dec_gain_grad,
        dec_shift_grad,
        grad_enc_qkv,
        grad_enc_attn_out,
        grad_enc_ffn_in,
        grad_enc_ffn_out,
        enc_gain_grad,
        enc_shift_grad,
    ) = lax.psum(
        (
            grad_mask_embed,
            grad_self_qkv,
            grad_self_out,
            grad_cross_qkv,
            grad_cross_out,
            grad_dec_ffn_in,
            grad_dec_ffn_out,
            dec_gain_grad,
            dec_shift_grad,
            grad_enc_qkv,
            grad_enc_attn_out,
            grad_enc_ffn_in,
            grad_enc_ffn_out,
            enc_gain_grad,
            enc_shift_grad,
        ),
        "dp",
    )
    gain_grads = jnp.concatenate([enc_gain_grad, dec_gain_grad], axis=0)
    shift_grads = jnp.concatenate([enc_shift_grad, dec_shift_grad], axis=0)
    return (
        encoded_low,
        decoded.astype(jnp.bfloat16),
        grad_enc_in,
        grad_dec_in,
        grad_mask_embed,
        grad_enc_qkv,
        grad_enc_attn_out,
        grad_enc_ffn_in,
        grad_enc_ffn_out,
        grad_self_qkv,
        grad_self_out,
        grad_cross_qkv,
        grad_cross_out,
        grad_dec_ffn_in,
        grad_dec_ffn_out,
        gain_grads,
        shift_grads,
    )


def solution(mesh):
    placed = (
        P("dp", None, None),
        P("dp", None, None),
        P("dp", None),
        P("dp", None),
        P("dp", None),
        P(),
        P(None, None, "tensor"),
        P("tensor", None),
        P(None, "tensor"),
        P("tensor", None),
        P(None, None, "tensor"),
        P("tensor", None),
        P(None, None, "tensor"),
        P("tensor", None),
        P(None, "tensor"),
        P("tensor", None),
        P(),
        P(),
        P("dp", None, None),
        P("dp", None, None),
    )
    return jax.shard_map(
        per_device,
        mesh=mesh,
        in_specs=placed,
        out_specs=(
            P("dp", None, None),
            P("dp", None, None),
            P("dp", None, None),
            P("dp", None, None),
            P(),
            P(None, None, "tensor"),
            P("tensor", None),
            P(None, "tensor"),
            P("tensor", None),
            P(None, None, "tensor"),
            P("tensor", None),
            P(None, None, "tensor"),
            P("tensor", None),
            P(None, "tensor"),
            P("tensor", None),
            P(),
            P(),
        ),
        check_vma=False,
    )
```

profile of v0, /device:TPU:17, one launch (start us, length us, event | category | flops | bytes accessed | tf_op | source)
XLA Modules:
  0.0 1283.1 jit_solution(7288275264529498845)
XLA Ops:
  38.4 73.2 %all-reduce.15.cloned.1.call-done = f32[1,1024,512]{2,1,0:T(8,128)} async-done(((f32[1,1024,512]{2,1,0:T(8,128)}), f32[1,1024,512]{2,1,0:T(8,128)}) %all-reduce.15.cloned.1.call-update) | async-done | bytes 2097168 | tf_op jit(solution)/shard_map/psum | solution.py:151
  115.2 6.4 multiply_convert_fusion.4
  125.0 154.4 %all-reduce.31.cloned.1.call-done = (f32[1,1024,512]{2,1,0:T(8,128)}, f32[1,1024,512]{2,1,0:T(8,128)}) async-done(((f32[1,1024,512]{2,1,0:T(8,128)}, f32[1,1024,512]{2,1,0:T(8,128)}), (f32[1,1024,512]{2,1,0:T(8,128)}, f32[1,1024,512]{2,1,0:T(8,128)})) %all-reduce.31.cloned.1.call-update) | async-done | bytes 4194320 | tf_op jit(solution)/shard_map/psum | solution.py:151
  299.2 85.4 %all-reduce.17.cloned.1.call-done = f32[1,1024,512]{2,1,0:T(8,128)} async-done(((f32[1,1024,512]{2,1,0:T(8,128)}), f32[1,1024,512]{2,1,0:T(8,128)}) %all-reduce.17.cloned.1.call-update) | async-done | bytes 2097168 | tf_op jit(solution)/shard_map/psum | solution.py:151
  388.9 6.4 multiply_convert_fusion.3
  398.7 85.2 %all-reduce.19.cloned.1.call-done = f32[1,1024,512]{2,1,0:T(8,128)} async-done(((f32[1,1024,512]{2,1,0:T(8,128)}), f32[1,1024,512]{2,1,0:T(8,128)}) %all-reduce.19.cloned.1.call-update) | async-done | bytes 2097168 | tf_op jit(solution)/shard_map/psum | solution.py:151
  497.1 84.4 %all-reduce.21.cloned.1.call-done = f32[1,1024,512]{2,1,0:T(8,128)} async-done(((f32[1,1024,512]{2,1,0:T(8,128)}), f32[1,1024,512]{2,1,0:T(8,128)}) %all-reduce.21.cloned.1.call-update) | async-done | bytes 2097168 | tf_op jit(solution)/shard_map/psum | solution.py:155
  581.6 5.5 multiply_reduce_fusion.3
  590.3 4.6 fusion.308
  597.4 14.4 %fusion.150 = bf16[2,64,1024]{2,1,0:T(8,128)(2,1)S(1)} fusion(bf16[1024,2,64]{0,2,1:T(8,128)(2,1)} %bitcast.373, f32[2,1024,1024]{1,2,0:T(8,128)} %fusion.308, f32[2,1024,1024]{1,2,0:T(8,128)} %copy-done.26, f32[2,1024]{1,0:T(2,128)} %log_add_fusion.2, pred[1024,1024]{0,1:T(8,128)(4,1)} %get-tuple-element.105), kind=kOutput, calls=%fused_computation.195 | convolution fusion | flops 291638272 | bytes 18358272 | tf_op jit(solution)/shard_map/rhqk,rqhc->rkhc/dot_general | solution.py:112
  614.3 15.4 %fusion.153 = bf16[2,64,1024]{2,1,0:T(8,128)(2,1)} fusion(bf16[1024,2,64]{0,2,1:T(8,128)(2,1)} %bitcast.371, f32[2,1024,1024]{1,2,0:T(8,128)} %fusion.308, f32[2,1024,1024]{1,2,0:T(8,128)} %copy-done.26, f32[2,1024]{1,0:T(2,128)} %log_add_fusion.2, pred[1024,1024]{0,1:T(8,128)(4,1)} %get-tuple-element.105), kind=kOutput, calls=%fused_computation.196 | convolution fusion | flops 291638272 | bytes 18358272 | tf_op jit(solution)/shard_map/rhqk,rkhc->rqhc/dot_general | solution.py:105
  632.5 67.2 %all-reduce.23.cloned.1.call-done = f32[1,1024,512]{2,1,0:T(8,128)} async-done(((f32[1,1024,512]{2,1,0:T(8,128)}), f32[1,1024,512]{2,1,0:T(8,128)}) %all-reduce.23.cloned.1.call-update) | async-done | bytes 2097168 | tf_op jit(solution)/shard_map/psum | solution.py:239
  725.9 140.6 %all-reduce.29.cloned.1.call-done = (f32[1,1024,512]{2,1,0:T(8,128)}, f32[1,1024,512]{2,1,0:T(8,128)}) async-done(((f32[1,1024,512]{2,1,0:T(8,128)}, f32[1,1024,512]{2,1,0:T(8,128)}), (f32[1,1024,512]{2,1,0:T(8,128)}, f32[1,1024,512]{2,1,0:T(8,128)})) %all-reduce.29.cloned.1.call-update) | async-done | bytes 4194320 | tf_op jit(solution)/shard_map/psum | solution.py:155
  866.5 6.2 multiply_reduce_fusion.4
  879.7 4.6 fusion.310
  887.6 14.5 %fusion.138 = bf16[2,64,1024]{2,1,0:T(8,128)(2,1)} fusion(bf16[1024,2,64]{0,2,1:T(8,128)(2,1)S(1)} %bitcast.416, f32[2,1024,1024]{1,2,0:T(8,128)} %fusion.310, f32[2,1024,1024]{1,2,0:T(8,128)} %copy-done.25, f32[2,1024]{1,0:T(2,128)S(1)} %log_add_fusion, pred[1024,1024]{0,1:T(8,128)(4,1)S(1)} %copy-done.31), kind=kOutput, calls=%fused_computation.191 | convolution fusion | flops 291638272 | bytes 18358272 | tf_op jit(solution)/shard_map/rhqk,rkhc->rqhc/dot_general | solution.py:105
  902.1 14.9 %fusion.141 = bf16[2,64,1024]{2,1,0:T(8,128)(2,1)} fusion(bf16[1024,2,64]{0,2,1:T(8,128)(2,1)S(1)} %bitcast.414, f32[2,1024,1024]{1,2,0:T(8,128)} %fusion.310, f32[2,1024,1024]{1,2,0:T(8,128)} %copy-done.25, f32[2,1024]{1,0:T(2,128)S(1)} %log_add_fusion, pred[1024,1024]{0,1:T(8,128)(4,1)S(1)} %copy-done.31), kind=kOutput, calls=%fused_computation.192 | convolution fusion | flops 291638272 | bytes 18358272 | tf_op jit(solution)/shard_map/rhqk,rqhc->rkhc/dot_general | solution.py:112
  917.0 4.6 fusion.309
  921.6 5.8 fusion.132
  927.5 16.4 %fusion.144 = bf16[2,64,1024]{2,1,0:T(8,128)(2,1)S(1)} fusion(bf16[1024,2,64]{0,2,1:T(8,128)(2,1)S(1)} %bitcast.369, f32[2,1024,1024]{1,2,0:T(8,128)} %fusion.309, f32[2,1024,1024]{1,2,0:T(8,128)} %copy-done.24, f32[2,1024]{1,0:T(2,128)} %copy-done.157, pred[1024,1024]{0,1:T(8,128)(4,1)S(1)} %copy-done.29), kind=kOutput, calls=%fused_computation.193 | convolution fusion | flops 291638272 | bytes 18358272 | tf_op jit(solution)/shard_map/rhqk,rkhc->rqhc/dot_general | solution.py:105
  944.0 14.1 %fusion.147 = bf16[2,64,1024]{2,1,0:T(8,128)(2,1)S(1)} fusion(bf16[1024,2,64]{0,2,1:T(8,128)(2,1)S(1)} %bitcast.367, f32[2,1024,1024]{1,2,0:T(8,128)} %fusion.309, f32[2,1024,1024]{1,2,0:T(8,128)} %copy-done.24, f32[2,1024]{1,0:T(2,128)S(1)} %copy-done.158, pred[1024,1024]{0,1:T(8,128)(4,1)S(1)} %copy-done.29), kind=kOutput, calls=%fused_computation.194 | convolution fusion | flops 291638272 | bytes 18358272 | tf_op jit(solution)/shard_map/rhqk,rqhc->rkhc/dot_general | solution.py:112
  971.8 110.2 %all-reduce.25.cloned.1.call-done = (f32[3,512,128]{1,2,0:T(8,128)}, f32[128,512]{1,0:T(8,128)}, f32[512,512]{1,0:T(8,128)}, f32[512,512]{1,0:T(8,128)}, f32[3,5...) async-done(((f32[3,512,128]{1,2,0:T(8,128)}, f32[128,512]{1,0:T(8,128)}, ...) | async-done | bytes 7340048 | tf_op jit(solution)/shard_map/psum | solution.py:293
  1084.2 155.6 %all-reduce.27.cloned.1.call-done = (f32[1,1024,512]{2,1,0:T(8,128)}, f32[1,1024,512]{2,1,0:T(8,128)}) async-done(((f32[1,1024,512]{2,1,0:T(8,128)}, f32[1,1024,512]{2,1,0:T(8,128)}), (f32[1,1024,512]{2,1,0:T(8,128)}, f32[1,1024,512]{2,1,0:T(8,128)})) %all-reduce.27.cloned.1.call-update) | async-done | bytes 4194320 | tf_op jit(solution)/shard_map/psum | solution.py:155
  1245.1 22.2 %all-reduce = (f32[512]{0:T(512)}, f32[3,512]{1,0:T(4,128)S(1)}, f32[2,512]{1,0:T(2,128)S(1)}, f32[3,512]{1,0:T(4,128)S(1)}, f32[2,512]{1,0:T(2,128)S(1)}) all-reduce(f32[512]{0:T(512)S(1)} %get-tuple-element.92, f32[3,512]{1,0:T(4,128)S(1)} %pad_maximum_fusion.5, ...), channel_id=1, replica_groups=mesh['dp'=8,'tensor'=4] {'dp'}, use_global_device_ids=true, to_apply=%region_41.42 | all-reduce | flops 5632 | bytes 45056 | tf_op jit(solution)/shard_map/psum | solution.py:293
  (505 shorter events, 154.8 us)
Async XLA Ops:
  7.2 381.7 %copy-start = (bf16[512,512]{1,0:T(8,128)(2,1)S(1)}, bf16[512,512]{1,0:T(8,128)(2,1)}, u32[]{:S(2)}) copy-start(bf16[512,512]{1,0:T(8,128)(2,1)} %param.34) | copy-start | bytes 1572868
  7.2 104.4 %all-reduce.15.cloned.1.call-start = ((), (), s32[]{:S(2)}) async-start(), calls=%async_computation | async-start | bytes 4194304 | tf_op jit(solution)/shard_map/psum | solution.py:151
  25.0 254.4 %all-reduce.31.cloned.1.call-start = ((), (), s32[]{:S(2)}) async-start(), calls=%async_computation.8 | async-start | bytes 8388608 | tf_op jit(solution)/shard_map/psum | solution.py:151
  37.8 241.6 %copy-start.111 = (f32[1,512]{1,0:T(1,128)}, f32[1,512]{1,0:T(1,128)S(1)}, u32[]{:S(2)}) copy-start(f32[1,512]{1,0:T(1,128)S(1)} %get-tuple-element.98) | copy-start | bytes 6148
  37.8 346.9 %copy-start.109 = (f32[1,512]{1,0:T(1,128)}, f32[1,512]{1,0:T(1,128)S(1)}, u32[]{:S(2)}) copy-start(f32[1,512]{1,0:T(1,128)S(1)} %get-tuple-element.96) | copy-start | bytes 6148
  114.2 165.2 %copy-start.98 = (f32[1024]{0:T(1024)}, f32[1024]{0:T(1024)S(1)}, u32[]{:S(2)}) copy-start(f32[1024]{0:T(1024)S(1)} %add_rsqrt_fusion.4) | copy-start | bytes 12292
  124.7 260.0 %all-reduce.17.cloned.1.call-start = ((), (), s32[]{:S(2)}) async-start(), calls=%async_computation.1 | async-start | bytes 4194304 | tf_op jit(solution)/shard_map/psum | solution.py:151
  286.6 98.1 %copy-start.100 = (f32[1024]{0:T(1024)}, f32[1024]{0:T(1024)S(1)}, u32[]{:S(2)}) copy-start(f32[1024]{0:T(1024)S(1)} %add_rsqrt_fusion.2) | copy-start | bytes 12292
  299.2 184.7 %all-reduce.19.cloned.1.call-start = ((), (), s32[]{:S(2)}) async-start(), calls=%async_computation.2 | async-start | bytes 4194304 | tf_op jit(solution)/shard_map/psum | solution.py:151
  398.3 183.2 %all-reduce.21.cloned.1.call-start = ((), (), s32[]{:S(2)}) async-start(), calls=%async_computation.3 | async-start | bytes 4194304 | tf_op jit(solution)/shard_map/psum | solution.py:155
  495.8 85.7 %copy-start.105 = (f32[1024]{0:T(1024)S(1)}, f32[1024]{0:T(1024)}, u32[]{:S(2)}) copy-start(f32[1024]{0:T(1024)} %copy-done.104) | copy-start | bytes 12292
  495.8 85.7 %copy-start.114 = (f32[1,512]{1,0:T(1,128)S(1)}, f32[1,512]{1,0:T(1,128)}, u32[]{:S(2)}) copy-start(f32[1,512]{1,0:T(1,128)} %get-tuple-element.99) | copy-start | bytes 6148
  495.8 85.7 %copy-start.116 = (f32[1024]{0:T(1024)S(1)}, f32[1024]{0:T(1024)}, u32[]{:S(2)}) copy-start(f32[1024]{0:T(1024)} %copy-done.115) | copy-start | bytes 12292
  495.8 85.7 %copy-start.135 = (f32[1,512]{1,0:T(1,128)S(1)}, f32[1,512]{1,0:T(1,128)}, u32[]{:S(2)}) copy-start(f32[1,512]{1,0:T(1,128)} %get-tuple-element.95) | copy-start | bytes 6148
  495.9 203.8 %all-reduce.23.cloned.1.call-start = ((), (), s32[]{:S(2)}) async-start(), calls=%async_computation.4 | async-start | bytes 4194304 | tf_op jit(solution)/shard_map/psum | solution.py:239
  614.1 252.4 %all-reduce.29.cloned.1.call-start = ((), (), s32[]{:S(2)}) async-start(), calls=%async_computation.7 | async-start | bytes 8388608 | tf_op jit(solution)/shard_map/psum | solution.py:155
  711.9 370.1 %all-reduce.25.cloned.1.call-start = ((), (), s32[]{:S(2)}) async-start(), calls=%async_computation.5 | async-start | bytes 14680064 | tf_op jit(solution)/shard_map/psum | solution.py:293
  712.6 209.0 %copy-start.157 = (f32[2,1024]{1,0:T(2,128)}, f32[2,1024]{1,0:T(2,128)S(1)}, u32[]{:S(2)}) copy-start(f32[2,1024]{1,0:T(2,128)S(1)} %log_add_fusion.1) | copy-start | bytes 24580
  724.2 142.3 %copy-start.99 = (f32[1024]{0:T(1024)S(1)}, f32[1024]{0:T(1024)}, u32[]{:S(2)}) copy-start(f32[1024]{0:T(1024)} %copy-done.98) | copy-start | bytes 12292
  724.2 142.3 %copy-start.101 = (f32[1024]{0:T(1024)S(1)}, f32[1024]{0:T(1024)}, u32[]{:S(2)}) copy-start(f32[1024]{0:T(1024)} %copy-done.100) | copy-start | bytes 12292
  724.2 142.3 %copy-start.110 = (f32[1,512]{1,0:T(1,128)S(1)}, f32[1,512]{1,0:T(1,128)}, u32[]{:S(2)}) copy-start(f32[1,512]{1,0:T(1,128)} %copy-done.109) | copy-start | bytes 6148
  724.2 142.3 %copy-start.112 = (f32[1,512]{1,0:T(1,128)S(1)}, f32[1,512]{1,0:T(1,128)}, u32[]{:S(2)}) copy-start(f32[1,512]{1,0:T(1,128)} %copy-done.111) | copy-start | bytes 6148
  964.4 275.5 %all-reduce.27.cloned.1.call-start = ((), (), s32[]{:S(2)}) async-start(), calls=%async_computation.6 | async-start | bytes 8388608 | tf_op jit(solution)/shard_map/psum | solution.py:155
  971.0 268.9 %copy-start.11 = (f32[1,1024,512]{2,1,0:T(8,128)S(1)}, f32[1,1024,512]{2,1,0:T(8,128)}, u32[]{:S(2)}) copy-start(f32[1,1024,512]{2,1,0:T(8,128)} %copy-done.10) | copy-start | bytes 6291460
  (165 other events, 1087.9 us)
Sparse Core Ops, SparseCore 0:
  25.1 86.4 all-reduce.14
  124.8 154.4 all-reduce.30
  299.3 85.3 all-reduce.16
  398.4 85.4 all-reduce.18
  496.0 85.4 all-reduce.20
  614.2 85.4 all-reduce.22
  712.0 154.4 all-reduce.28
  964.5 117.3 all-reduce.24
  1085.0 154.8 all-reduce.26
where the time goes:
time: 1290 us; the launch traced here: 1280 us
  waiting for transfers between devices  956 us (74%)
  matrix products  197 us (15%)
  other arithmetic  54.4 us (4%)
  local copies, waits for them, and re-layouts  35.4 us (3%)
  blocking collectives  22.2 us (2%)
  between operations  16.1 us (1%)
    psum x4, waiting for transfers between devices, sublayer_total(): return lax.psum(partial_value, 'tensor')  398 us
    psum x3, waiting for transfers between devices, input_total(): return lax.psum(partial_value, 'tensor')  381 us
    psum x1, waiting for transfers between devices, per_device(): lax.psum((grad_mask_embed, grad_self_qkv, grad_self_out, grad_cross_qkv,...  110 us
    psum x1, waiting for transfers between devices, per_device(): query_total, key_total = lax.psum((query_part, key_part), 'tensor')  67.2 us
    dot_general x3, matrix products, attend_backward(): jnp.einsum('rhqk,rkhc->rqhc', grad_raw, split_heads(keys), preferred_elem...  46.3 us
    dot_general x3, matrix products, attend_backward(): jnp.einsum('rhqk,rqhc->rkhc', grad_raw, split_heads(queries), preferred_e...  43.4 us
    unnamed x370, local copies, waits for them, and re-layouts  34.2 us
    dot_general x16, matrix products, project(): jnp.einsum('rld,de->rle', inputs, weight, preferred_element_type=jnp.floa...  30.7 us
  transfers between devices with their start and end apart: 9, of which 9 were waited for; matrix products, arithmetic and copies ran while one was open for 4% of the time, Pallas kernels for 0%

commit v1 on v0

v1 whole, which is shorter than its diff:
```python
import functools

import jax
import jax.numpy as jnp
from jax import lax
from jax.experimental import pallas as pl
from jax.experimental.pallas import tpu as pltpu
from jax.sharding import PartitionSpec as P

f32, bf16 = jnp.float32, jnp.bfloat16
HEAD_DIM = 64
EPS = 1e-05
FLOOR = -1000000000.0
BLK = 256
MB = 1 << 20
MESH = pl.DeviceIdType.MESH
VM = pltpu.VMEM


def nt(a, b):
    return lax.dot_general(a, b, (((1,), (1,)), ((), ())), preferred_element_type=f32)


def nn(a, b):
    return lax.dot_general(a, b, (((1,), (0,)), ((), ())), preferred_element_type=f32)


def tn(a, b):
    return lax.dot_general(a, b, (((0,), (0,)), ((), ())), preferred_element_type=f32)


def layer_norm(v):
    c = v - jnp.mean(v, axis=-1, keepdims=True)
    r = lax.rsqrt(jnp.mean(c * c, axis=-1, keepdims=True) + EPS)
    return c * r, r


def layer_norm_back(dy, n, r, gain):
    dn = dy * gain
    m1 = jnp.mean(dn, axis=-1, keepdims=True)
    m2 = jnp.mean(dn * n, axis=-1, keepdims=True)
    return r * (dn - m1 - n * m2)


def build(dst, own, land, kinds, rows):
    for k in range(kinds):
        size = own.shape[1]
        dst[k, :size] = own[k]
        rest = land[:, k * rows : (k + 1) * rows, :].reshape(24 * rows, land.shape[2])
        dst[k, size:] = rest.astype(bf16)


def block_diag(a, b):
    z = jnp.zeros_like(a)
    return jnp.concatenate(
        [jnp.concatenate([a, z], axis=1), jnp.concatenate([z, b], axis=1)], axis=0
    )


def two_heads(x):
    lane = lax.broadcasted_iota(jnp.int32, x.shape, 1)
    z = jnp.zeros_like(x)
    return jnp.concatenate([jnp.where(lane < HEAD_DIM, x, z), jnp.where(lane < HEAD_DIM, z, x)], 0)


def window(i, win, width, cross):
    if width == 1024:
        return 0
    if cross:
        return pl.multiple_of(win[i], 128)
    return pl.multiple_of(jnp.clip(i * BLK - 128, 0, 512), 128)


def attend_fwd(cross, from_norm, *refs):
    (win, x, xg, xs, blow, pq, pk, own, land, gain, shift) = refs[:11]
    (n_o, r_o, y_o, pt_o, q_o, v_o, kt_o, ot_o) = refs[11:19]
    (wt, k_s, vt_s) = refs[19:]
    i = pl.program_id(0)

    @pl.when(i == 0)
    def _():
        build(wt, own, land, 4, 16)
        for b in range(4):
            rows = slice(b * BLK, (b + 1) * BLK)
            kb = blow[rows]
            k_s[rows] = nt(kb, wt[1]).astype(bf16)
            v_o[rows] = nt(kb, wt[2]).astype(bf16)
            kt_o[:, rows] = nt(wt[1], kb).astype(bf16)
            vt_s[:, rows] = nt(wt[2], kb).astype(bf16)

    xv = x[...].astype(f32)
    if from_norm:
        xv = xv * xg[...] + xs[...]
    xl = xv.astype(bf16)
    qt = (nt(wt[0], xl) * 0.125).astype(bf16)
    q_o[...] = (nt(xl, wt[0]) * 0.125).astype(bf16)

    def heads(width):
        start = window(i, win, width, cross)
        keys = pl.ds(start, width)
        bias = jnp.where(pk[keys] == pq[...], 0.0, FLOOR).astype(f32)
        bias = jnp.concatenate([bias, bias], axis=1)
        for p in range(4):
            lanes = slice(p * 128, p * 128 + 128)
            rhs = block_diag(qt[p * 128 : p * 128 + 64], qt[p * 128 + 64 : p * 128 + 128])
            s = nn(k_s[keys, lanes], rhs) + bias
            e = jnp.exp(s - jnp.max(s, axis=0, keepdims=True))
            pt = (e * (1.0 / jnp.sum(e, axis=0, keepdims=True))).astype(bf16)
            pt_o[0, p, :width] = pt
            for h in range(2):
                ch = slice(p * 128 + h * 64, p * 128 + h * 64 + 64)
                ot_o[ch] = nn(vt_s[ch, keys], pt[:, h * BLK : (h + 1) * BLK]).astype(bf16)

    if cross:
        pl.when(win[4 + i] == 0)(lambda: heads(512))
        pl.when(win[4 + i] != 0)(lambda: heads(1024))
    else:
        heads(512)
    n, r = layer_norm(xv + tn(ot_o[...], wt[3]))
    n_o[...] = n
    r_o[...] = r
    y_o[...] = (n * gain[...] + shift[...]).astype(bf16)


def attend_bwd(cross, *refs):
    (win, dy, n, r, gain, own, land, pt, v, kt, q, ot, alow, blow) = refs[:14]
    if cross:
        dx_o, dkey_o, dqkv_o, dwo_o, gs_o = refs[14:19]
        wt, dk_s, dv_s = refs[19:]
    else:
        dx_o, dqkv_o, dwo_o, gs_o = refs[14:18]
        wt, dk_s, dv_s = refs[18:]
    i = pl.program_id(0)

    @pl.when(i == 0)
    def _():
        build(wt, own, land, 4, 16)
        dk_s[...] = jnp.zeros_like(dk_s)
        dv_s[...] = jnp.zeros_like(dv_s)
        dqkv_o[...] = jnp.zeros_like(dqkv_o)
        dwo_o[...] = jnp.zeros_like(dwo_o)
        gs_o[...] = jnp.zeros_like(gs_o)

    dyv, nv = dy[...], n[...]
    gs_o[0:1] += jnp.sum(dyv * nv, axis=0, keepdims=True)
    gs_o[1:2] += jnp.sum(dyv, axis=0, keepdims=True)
    d = layer_norm_back(dyv, nv, r[...], gain[...])
    g = d.astype(bf16)
    do = nt(g, wt[3]).astype(bf16)
    dot = nt(wt[3], g).astype(bf16)
    otv = ot[...]
    prod = dot.astype(f32) * otv.astype(f32)
    dqt = []

    def heads(width):
        start = window(i, win, width, cross)
        keys = pl.ds(start, width)
        rows = []
        for p in range(4):
            lanes = slice(p * 128, p * 128 + 128)
            a = slice(p * 128, p * 128 + 64)
            b = slice(p * 128 + 64, p * 128 + 128)
            delta = jnp.concatenate(
                [jnp.sum(prod[a], axis=0, keepdims=True), jnp.sum(prod[b], axis=0, keepdims=True)],
                axis=1,
            )
            dpt = nn(v[keys, lanes], block_diag(dot[a], dot[b]))
            ptv = pt[0, p, :width]
            dst = (ptv.astype(f32) * (dpt - delta)).astype(bf16)
            dv_s[keys, lanes] += nn(ptv, two_heads(do[:, lanes]))
            dk_s[keys, lanes] += nn(dst, two_heads(q[:, lanes]))
            rows.append((nn(kt[a, keys], dst[:, :BLK]) * 0.125).astype(bf16))
            rows.append((nn(kt[b, keys], dst[:, BLK:]) * 0.125).astype(bf16))
        dqt = jnp.concatenate(rows, axis=0)
        dqkv_o[0] += nn(dqt[:128], alow[...])
        dx = d + tn(dqt, wt[0])
        if cross:
            dx_o[...] = dx
        else:
            dx_o[pl.ds(pl.multiple_of(i * BLK, BLK), BLK)] = dx

    if cross:
        pl.when(win[4 + i] == 0)(lambda: heads(512))
        pl.when(win[4 + i] != 0)(lambda: heads(1024))
    else:
        heads(512)
    dwo_o[...] += nn(otv[:128], g)

    @pl.when(i == 3)
    def _():
        for b in range(4):
            rows = slice(b * BLK, (b + 1) * BLK)
            dkb, dvb = dk_s[rows].astype(bf16), dv_s[rows].astype(bf16)
            kx = nn(dkb, wt[1]) + nn(dvb, wt[2])
            if cross:
                dkey_o[rows] = kx
            else:
                dx_o[rows] += kx
            bl = blow[rows]
            dqkv_o[1] += tn(dkb[:, :128], bl)
            dqkv_o[2] += tn(dvb[:, :128], bl)


def ffn_fwd(*refs):
    (np_, gp_, sp_, alow, own, land, gain, shift) = refs[:8]
    (n_o, r_o, y_o, h_o, slope_o) = refs[8:13]
    (w,) = refs[13:]
    i = pl.program_id(0)

    @pl.when(i == 0)
    def _():
        build(w, own, land, 2, 64)

    acc = np_[...] * gp_[...] + sp_[...]
    al = alow[...]
    for c in range(4):
        hid = slice(c * 512, (c + 1) * 512)
        before = nt(al, w[0, hid])
        cdf = 0.5 + 0.5 * lax.erf(before * (0.5**0.5))
        pdf = jnp.exp(before * before * -0.5) * 0.3989422804014327
        slope_o[:, hid] = (cdf + before * pdf).astype(bf16)
        hidden = (before * cdf).astype(bf16)
        if c == 0:
            h_o[...] = hidden
        acc += nn(hidden, w[1, hid])
    n, r = layer_norm(acc)
    n_o[...] = n
    r_o[...] = r
    y_o[...] = (n * gain[...] + shift[...]).astype(bf16)


def ffn_bwd(two_dy, *refs):
    if two_dy:
        (dy, dy2, n, r, gain, alow, own, land, h, slope) = refs[:10]
        refs = refs[10:]
    else:
        (dy, n, r, gain, alow, own, land, h, slope) = refs[:9]
        refs = refs[9:]
    (dx_o, dw1_o, dw2_o, gs_o, w) = refs
    i = pl.program_id(0)

    @pl.when(i == 0)
    def _():
        build(w, own, land, 2, 64)
        dw1_o[...] = jnp.zeros_like(dw1_o)
        dw2_o[...] = jnp.zeros_like(dw2_o)
        gs_o[...] = jnp.zeros_like(gs_o)

    dyv, nv = dy[...].astype(f32), n[...]
    if two_dy:
        dyv = dyv + dy2[...]
    gs_o[0:1] += jnp.sum(dyv * nv, axis=0, keepdims=True)
    gs_o[1:2] += jnp.sum(dyv, axis=0, keepdims=True)
    d = layer_norm_back(dyv, nv, r[...], gain[...])
    g = d.astype(bf16)
    acc = d
    for c in range(4):
        hid = slice(c * 512, (c + 1) * 512)
        db = (nt(g, w[1, hid]) * slope[:, hid].astype(f32)).astype(bf16)
        acc += nn(db, w[0, hid])
        if c == 0:
            dw1_o[...] += tn(alow[...], db)
            dw2_o[...] += tn(h[...], g)
    dx_o[...] = acc


def whole(shape):
    return pl.BlockSpec(shape, lambda i: (0,) * len(shape))


def rows_of(width):
    return pl.BlockSpec((BLK, width), lambda i: (i, 0))


SDS = jax.ShapeDtypeStruct
SMEM_SPEC = pl.BlockSpec(memory_space=pltpu.SMEM)
PARAMS = pltpu.CompilerParams(vmem_limit_bytes=60 * MB)


def call_attend_fwd(cross, from_norm, win, x, xg, xs, blow, pq, pk, own, land, gain, shift):
    width = 1024 if cross else 512
    return pl.pallas_call(
        functools.partial(attend_fwd, cross, from_norm),
        grid=(4,),
        in_specs=[
            SMEM_SPEC,
            rows_of(512),
            whole((1, 512)),
            whole((1, 512)),
            whole((1024, 512)),
            pl.BlockSpec((1, BLK), lambda i: (0, i)),
            whole((1024, 1)),
            whole((4, 128, 512)),
            whole((24, 64, 512)),
            whole((1, 512)),
            whole((1, 512)),
        ],
        out_specs=[
            rows_of(512),
            rows_of(1),
            rows_of(512),
            pl.BlockSpec((1, 4, width, 512), lambda i: (i, 0, 0, 0)),
            rows_of(512),
            whole((1024, 512)),
            whole((512, 1024)),
            pl.BlockSpec((512, BLK), lambda i: (0, i)),
        ],
        out_shape=[
            SDS((1024, 512), f32),
            SDS((1024, 1), f32),
            SDS((1024, 512), bf16),
            SDS((4, 4, width, 512), bf16),
            SDS((1024, 512), bf16),
            SDS((1024, 512), bf16),
            SDS((512, 1024), bf16),
            SDS((512, 1024), bf16),
        ],
        scratch_shapes=[VM((4, 512, 512), bf16), VM((1024, 512), bf16), VM((512, 1024), bf16)],
        compiler_params=PARAMS,
    )(win, x, xg, xs, blow, pq, pk, own, land, gain, shift)


def call_attend_bwd(cross, win, dy, n, r, gain, own, land, saved, alow, blow):
    pt, q, v, kt, ot = saved
    width = 1024 if cross else 512
    dx_specs = [rows_of(512), whole((1024, 512))] if cross else [whole((1024, 512))]
    return pl.pallas_call(
        functools.partial(attend_bwd, cross),
        grid=(4,),
        in_specs=[
            SMEM_SPEC,
            rows_of(512),
            rows_of(512),
            rows_of(1),
            whole((1, 512)),
            whole((4, 128, 512)),
            whole((24, 64, 512)),
            pl.BlockSpec((1, 4, width, 512), lambda i: (i, 0, 0, 0)),
            whole((1024, 512)),
            whole((512, 1024)),
            rows_of(512),
            pl.BlockSpec((512, BLK), lambda i: (0, i)),
            rows_of(512),
            whole((1024, 512)),
        ],
        out_specs=dx_specs + [whole((3, 128, 512)), whole((128, 512)), whole((8, 512))],
        out_shape=[SDS((1024, 512), f32)] * len(dx_specs)
        + [SDS((3, 128, 512), f32), SDS((128, 512), f32), SDS((8, 512), f32)],
        scratch_shapes=[VM((4, 512, 512), bf16), VM((1024, 512), f32), VM((1024, 512), f32)],
        compiler_params=PARAMS,
    )(win, dy, n, r, gain, own, land, pt, v, kt, q, ot, alow, blow)


def call_ffn_fwd(n, g, s, alow, own, land, gain, shift):
    return pl.pallas_call(
        ffn_fwd,
        grid=(4,),
        in_specs=[
            rows_of(512),
            whole((1, 512)),
            whole((1, 512)),
            rows_of(512),
            whole((2, 512, 512)),
            whole((24, 128, 512)),
            whole((1, 512)),
            whole((1, 512)),
        ],
        out_specs=[rows_of(512), rows_of(1), rows_of(512), rows_of(512), rows_of(2048)],
        out_shape=[
            SDS((1024, 512), f32),
            SDS((1024, 1), f32),
            SDS((1024, 512), bf16),
            SDS((1024, 512), bf16),
            SDS((1024, 2048), bf16),
        ],
        scratch_shapes=[VM((2, 2048, 512), bf16)],
        compiler_params=PARAMS,
    )(n, g, s, alow, own, land, gain, shift)


def call_ffn_bwd(dys, n, r, gain, alow, own, land, h, slope):
    return pl.pallas_call(
        functools.partial(ffn_bwd, len(dys) == 2),
        grid=(4,),
        in_specs=[rows_of(512)] * len(dys)
        + [
            rows_of(512),
            rows_of(1),
            whole((1, 512)),
            rows_of(512),
            whole((2, 512, 512)),
            whole((24, 128, 512)),
            rows_of(512),
            rows_of(2048),
        ],
        out_specs=[rows_of(512), whole((512, 512)), whole((512, 512)), whole((8, 512))],
        out_shape=[
            SDS((1024, 512), f32),
            SDS((512, 512), f32),
            SDS((512, 512), f32),
            SDS((8, 512), f32),
        ],
        scratch_shapes=[VM((2, 2048, 512), bf16)],
        compiler_params=PARAMS,
    )(*dys, n, r, gain, alow, own, land, h, slope)


def plane_index():
    dp = lax.axis_index("dp")
    return dp, lax.rem(dp, 8)


def barrier_with(peers):
    sem = pltpu.get_barrier_semaphore()
    for peer in peers:
        pl.semaphore_signal(sem, inc=1, device_id=peer, device_id_type=MESH)
    pl.semaphore_wait(sem, len(peers))


def gather_kernel(tn_, groups, *refs):
    own, land = refs[:groups], refs[groups : 2 * groups]
    zs, zr, ps, pr = refs[2 * groups :]
    dp = lax.axis_index("dp")
    z = lax.axis_index("tensor")
    core = dp + 1 - 2 * lax.rem(dp, 2)
    xn = dp + 2 - 4 * lax.rem(lax.div(dp, 2), 2)
    yn = dp + 4 - 8 * lax.rem(lax.div(dp, 4), 2)
    zn = [lax.rem(z + k, tn_) for k in range(1, tn_)]
    barrier_with([(core, z), (xn, z), (yn, z)] + [(dp, k) for k in zn])

    def copy(src, dst, ss, rs, dev):
        return pltpu.make_async_remote_copy(
            src_ref=src, dst_ref=dst, send_sem=ss, recv_sem=rs, device_id=dev, device_id_type=MESH
        )

    first = []
    for g in range(groups):
        cs = [
            copy(own[g], land[g].at[k - 1, 0, 0], zs.at[g, k - 1], zr.at[g, k - 1],
                 (dp, lax.rem(z + tn_ - k, tn_)))
            for k in range(1, tn_)
        ]
        for c in cs:
            c.start()
        first.append(cs)

    second, third, pairs = [], [], []
    def stage2(g):
        for c in first[g]:
            c.wait_recv()
        l = land[g]
        cs = [
            copy(l.at[:, 0, 0], l.at[:, 0, 1], ps.at[g, 0], pr.at[g, 0], (xn, z)),
            copy(l.at[:, 0, 0], l.at[:, 0, 2], ps.at[g, 1], pr.at[g, 1], (yn, z)),
            copy(l.at[:, 0, 0], l.at[:, 1, 0], ps.at[g, 2], pr.at[g, 2], (core, z)),
        ]
        for c in cs:
            c.start()
        second.append(cs)

    def stage3(g):
        half = own[g].shape[0] // 2
        l = land[g]
        a, b = pl.ds(0, half), pl.ds(half, half)
        cs = [
            copy(l.at[:, 0, 1, a], l.at[:, 0, 3, a], ps.at[g, 3], pr.at[g, 3], (yn, z)),
            copy(l.at[:, 0, 2, b], l.at[:, 0, 3, b], ps.at[g, 4], pr.at[g, 4], (xn, z)),
            copy(l.at[:, 0, 1], l.at[:, 1, 1], ps.at[g, 5], pr.at[g, 5], (core, z)),
            copy(l.at[:, 0, 2], l.at[:, 1, 2], ps.at[g, 6], pr.at[g, 6], (core, z)),
        ]
        second[g][0].wait_recv()
        cs[0].start()
        cs[2].start()
        second[g][1].wait_recv()
        cs[1].start()
        cs[3].start()
        third.append(cs)

    def stage4(g):
        l = land[g]
        third[g][0].wait_recv()
        third[g][1].wait_recv()
        c = copy(l.at[:, 0, 3], l.at[:, 1, 3], ps.at[g, 7], pr.at[g, 7], (core, z))
        c.start()
        pairs.append(c)

    for t in range(groups + 2):
        if t < groups:
            stage2(t)
        if 0 <= t - 1 < groups:
            stage3(t - 1)
        if 0 <= t - 2 < groups:
            stage4(t - 2)
    for g in range(groups):
        second[g][2].wait_recv()
        third[g][2].wait_recv()
        third[g][3].wait_recv()
        pairs[g].wait_recv()
        for c in first[g] + second[g] + third[g] + [pairs[g]]:
            c.wait_send()


def gather_weights(tn_, blobs):
    groups = len(blobs)
    return pl.pallas_call(
        functools.partial(gather_kernel, tn_, groups),
        in_specs=[pl.BlockSpec(memory_space=pl.ANY)] * groups,
        out_specs=[pl.BlockSpec(memory_space=pl.ANY)] * groups,
        out_shape=[SDS((3, 2, 4) + b.shape, f32) for b in blobs],
        scratch_shapes=[
            pltpu.SemaphoreType.DMA((groups, 3)),
            pltpu.SemaphoreType.DMA((groups, 3)),
            pltpu.SemaphoreType.DMA((groups, 8)),
            pltpu.SemaphoreType.DMA((groups, 8)),
        ],
        compiler_params=pltpu.CompilerParams(collective_id=0, has_side_effects=True),
    )(*blobs)


def sum_kernel(count, *refs):
    part, out = refs[:count], refs[count : 2 * count]
    got_c, got_a, got_b, got_a2, got_b2, held = (
        refs[2 * count + k * count : 2 * count + (k + 1) * count] for k in range(6)
    )
    ss, rs = refs[8 * count :]
    dp, j = plane_index()
    z = lax.axis_index("tensor")
    c, x, y = lax.rem(j, 2), lax.rem(lax.div(j, 2), 2), lax.div(j, 4)
    cn, xn, yn = (dp + 1 - 2 * c, z), (dp + 2 - 4 * x, z), (dp + 4 - 8 * y, z)
    barrier_with([cn, xn, yn])

    def copy(k, s, src, dst, dev):
        return pltpu.make_async_remote_copy(
            src_ref=src, dst_ref=dst, send_sem=ss.at[k, s], recv_sem=rs.at[k, s],
            device_id=dev, device_id_type=MESH,
        )

    every = []

    def go(cp):
        cp.start()
        every.append(cp)
        return cp

    halves = []
    for k in range(count):
        h = part[k].shape[3] // 2
        halves.append((pl.ds(0, h), pl.ds(h, h)))
    s0 = [go(copy(k, 0, part[k].at[:, :, 1 - c], got_c[k], cn)) for k in range(count)]
    s1 = []
    for k in range(count):
        a, b = halves[k]
        s0[k].wait_recv()
        held[k][...] = part[k][:, :, c] + got_c[k][...]
        s1.append((
            go(copy(k, 1, held[k].at[:, 1 - x, a], got_a[k], xn)),
            go(copy(k, 2, held[k].at[1 - y, :, b], got_b[k], yn)),
        ))
    s2 = []
    for k in range(count):
        a, b = halves[k]
        s1[k][0].wait_recv()
        held[k][:, x, a] += got_a[k][...]
        s1[k][1].wait_recv()
        held[k][y, :, b] += got_b[k][...]
        s2.append((
            go(copy(k, 3, held[k].at[1 - y, x, a], got_a2[k], yn)),
            go(copy(k, 4, held[k].at[y, 1 - x, b], got_b2[k], xn)),
        ))
    s3 = []
    for k in range(count):
        a, b = halves[k]
        o = out[k]
        s2[k][0].wait_recv()
        o[y, x, c, a] = held[k][y, x, a] + got_a2[k][...]
        s2[k][1].wait_recv()
        o[y, x, c, b] = held[k][y, x, b] + got_b2[k][...]
        s3.append((
            go(copy(k, 5, o.at[y, x, c, a], o.at[y, x, c, a], yn)),
            go(copy(k, 6, o.at[y, x, c, b], o.at[y, x, c, b], xn)),
        ))
    s4 = []
    for k in range(count):
        a, b = halves[k]
        o = out[k]
        s3[k][0].wait_recv()
        s3[k][1].wait_recv()
        s4.append((
            go(copy(k, 7, o.at[:, x, c, a], o.at[:, x, c, a], xn)),
            go(copy(k, 8, o.at[y, :, c, b], o.at[y, :, c, b], yn)),
        ))
    s5 = []
    for k in range(count):
        o = out[k]
        s4[k][0].wait_recv()
        s4[k][1].wait_recv()
        s5.append(go(copy(k, 9, o.at[:, :, c], o.at[:, :, c], cn)))
    for k in range(count):
        s5[k].wait_recv()
    for cp in every:
        cp.wait_send()


def sum_over_plane(parts):
    count = len(parts)
    shapes = [p.shape[3:] for p in parts]

    def bufs(lead, cut):
        return [VM(lead + (r // cut, w), f32) for r, w in shapes]

    return pl.pallas_call(
        functools.partial(sum_kernel, count),
        in_specs=[pl.BlockSpec(memory_space=pltpu.VMEM)] * count,
        out_specs=[pl.BlockSpec(memory_space=pltpu.VMEM)] * count,
        out_shape=[SDS(p.shape, f32) for p in parts],
        scratch_shapes=bufs((2, 2), 1) + bufs((2,), 2) + bufs((2,), 2) + bufs((), 2) + bufs((), 2)
        + bufs((2, 2), 1)
        + [pltpu.SemaphoreType.DMA((count, 10)), pltpu.SemaphoreType.DMA((count, 10))],
        compiler_params=pltpu.CompilerParams(
            collective_id=1, has_side_effects=True, vmem_limit_bytes=60 * MB
        ),
    )(*parts)


def attn_slices(qkv, out_w, j):
    own = jnp.concatenate([jnp.transpose(qkv, (0, 2, 1)), out_w[None]], axis=0)
    parts = own.reshape(4, 2, 4, 16, own.shape[2])
    piece = lax.dynamic_slice(
        parts, (0, lax.rem(j, 2), lax.div(j, 2), 0, 0), (4, 1, 1, 16, own.shape[2])
    )
    return own, piece.reshape(64, own.shape[2]).astype(f32)


def ffn_slices(w_in, w_out, j):
    own = jnp.stack([w_in.T, w_out])
    parts = own.reshape(2, 8, 64, own.shape[2])
    piece = lax.dynamic_slice(parts, (0, j, 0, 0), (2, 1, 64, own.shape[2]))
    return own, piece.reshape(128, own.shape[2]).astype(f32)


def cross_windows(source, target):
    low, high = target[0, ::BLK], target[0, BLK - 1 :: BLK]
    begin = jnp.sum((source[0][None, :] < low[:, None]).astype(jnp.int32), axis=1)
    end = jnp.sum((source[0][None, :] <= high[:, None]).astype(jnp.int32), axis=1)
    start = jnp.minimum(begin // 128 * 128, 512)
    return jnp.concatenate([start, (end - start > 512).astype(jnp.int32)])


def per_device(planes, tn_, enc_in, dec_in, src_idx, tgt_idx, masked, mask_embed, enc_qkv, enc_out_w,
               enc_w1, enc_w2, self_qkv, self_out_w, cross_qkv, cross_out_w, dec_w1, dec_w2,
               gains, shifts, enc_cot, dec_cot):
    _, j = plane_index()
    own_e, blob_e = attn_slices(enc_qkv, enc_out_w, j)
    own_s, blob_s = attn_slices(self_qkv, self_out_w, j)
    own_c, blob_c = attn_slices(cross_qkv, cross_out_w, j)
    own_f, blob_f = ffn_slices(enc_w1, enc_w2, j)
    own_d, blob_d = ffn_slices(dec_w1, dec_w2, j)
    lands = gather_weights(tn_, [blob_e, blob_f, blob_s, blob_c, blob_d])
    land_e, land_f, land_s, land_c, land_d = [a.reshape((24,) + a.shape[3:]) for a in lands]

    x_e, x_d = enc_in[0], dec_in[0]
    is_masked = (masked[0] == 1)[:, None]
    target = jnp.where(is_masked, mask_embed[None, :], x_d.astype(f32))
    target_low = target.astype(bf16)
    src_col, tgt_col = src_idx.reshape(1024, 1), tgt_idx.reshape(1024, 1)
    win = cross_windows(src_idx, tgt_idx)
    g = [gains[k : k + 1] for k in range(5)]
    s = [shifts[k : k + 1] for k in range(5)]

    n0, r0, first_low, *save_e = call_attend_fwd(
        False, False, win, x_e, g[0], s[0], x_e, src_idx, src_col, own_e, land_e, g[0], s[0])
    n1, r1, enc_low, h_e, slope_e = call_ffn_fwd(
        n0, g[0], s[0], first_low, own_f, land_f, g[1], s[1])
    n2, r2, second_low, *save_s = call_attend_fwd(
        False, False, win, target, g[2], s[2], target_low, tgt_idx, tgt_col, own_s, land_s, g[2], s[2])
    n3, r3, third_low, *save_c = call_attend_fwd(
        True, True, win, n2, g[2], s[2], enc_low, tgt_idx, src_col, own_c, land_c, g[3], s[3])
    n4, r4, dec_low, h_d, slope_d = call_ffn_fwd(
        n3, g[3], s[3], third_low, own_d, land_d, g[4], s[4])

    d_third, dw1_d, dw2_d, gs4 = call_ffn_bwd(
        [dec_cot[0]], n4, r4, g[4], third_low, own_d, land_d, h_d, slope_d)
    d_second, d_key, dqkv_c, dwo_c, gs3 = call_attend_bwd(
        True, win, d_third, n3, r3, g[3], own_c, land_c, save_c, second_low, enc_low)
    d_target, dqkv_s, dwo_s, gs2 = call_attend_bwd(
        False, win, d_second, n2, r2, g[2], own_s, land_s, save_s, target_low, target_low)
    d_first, dw1_e, dw2_e, gs1 = call_ffn_bwd(
        [enc_cot[0], d_key], n1, r1, g[1], first_low, own_f, land_f, h_e, slope_e)
    d_enc, dqkv_e, dwo_e, gs0 = call_attend_bwd(
        False, win, d_first, n0, r0, g[0], own_e, land_e, save_e, x_e, x_e)

    dec_grad = jnp.where(is_masked, 0.0, d_target)
    mask_grad = jnp.sum(jnp.where(is_masked, d_target, 0.0), axis=0)
    small = jnp.concatenate([mask_grad[None]] + [a[:2] for a in (gs0, gs1, gs2, gs3, gs4)])
    small = jnp.pad(small, ((0, 21), (0, 0))).reshape(2, 2, 2, 16, 128)

    def chunks(a):
        return a.reshape(2, 2, 2, a.size // 4096, 512)

    mats = [dqkv_e, dwo_e, dw1_e, dw2_e, dqkv_s, dwo_s, dqkv_c, dwo_c, dw1_d, dw2_d]
    sums = sum_over_plane([chunks(a) for a in mats] + [small])
    if planes > 1:
        same = [[p * 8 + k for p in range(planes)] for k in range(8)]
        sums = lax.psum(sums, "dp", axis_index_groups=same)
    dqkv_e, dwo_e, dw1_e, dw2_e, dqkv_s, dwo_s, dqkv_c, dwo_c, dw1_d, dw2_d = [
        a.reshape(m.shape) for a, m in zip(sums, mats)]
    dqkv_e, dqkv_s, dqkv_c = [jnp.transpose(a, (0, 2, 1)) for a in (dqkv_e, dqkv_s, dqkv_c)]
    small = sums[-1].reshape(32, 512)
    return (
        enc_low[None],
        dec_low[None],
        d_enc[None],
        dec_grad[None],
        small[0],
        dqkv_e,
        dwo_e,
        dw1_e,
        dw2_e,
        dqkv_s,
        dwo_s,
        dqkv_c,
        dwo_c,
        dw1_d,
        dw2_d,
        small[1:11:2],
        small[2:12:2],
    )


def solution(mesh):
    tokens, index = P("dp", None, None), P("dp", None)
    qkv, cols, rows = P(None, None, "tensor"), P(None, "tensor"), P("tensor", None)
    weights = (qkv, rows, cols, rows, qkv, rows, qkv, rows, cols, rows)
    return jax.shard_map(
        functools.partial(per_device, mesh.shape["dp"] // 8, mesh.shape["tensor"]),
        mesh=mesh,
        in_specs=(tokens, tokens, index, index, index, P()) + weights + (P(), P(), tokens, tokens),
        out_specs=(tokens,) * 4 + (P(),) + weights + (P(), P()),
        check_vma=False,
    )
```

time: 1290 us -> 455 us (0.35)
  waiting for transfers between devices: 956 us -> 0 us
  Pallas kernels: 0 us -> 409 us
  matrix products: 197 us -> 0 us
  other arithmetic: 54.4 us -> 15.9 us
  blocking collectives: 22.2 us -> 0 us
  between operations: 16.1 us -> 1.15 us
    psum x9 -> x0, waiting for transfers between devices: 956 us -> none  [the longest x4 398 us: sublayer_total(): return lax.psum(partial_value, 'tensor')]
    pallas_call x0 -> x12, Pallas kernels: none -> 409 us  [the longest x1 145 us: gather_weights(): pl.pallas_call(functools.partial(gather_kernel, tn_, groups), in_specs=[p...]
    dot_general x66 -> x0, matrix products: 197 us -> none  [the longest x3 46.3 us: attend_backward(): jnp.einsum('rhqk,rkhc->rqhc', grad_raw, split_heads(keys), preferred_elem...]
    reduce_sum x18 -> x2, other arithmetic: 38.3 us -> 2.52 us  [the longest x1 1.61 us: per_device(): mask_grad = jnp.sum(jnp.where(is_masked, d_target, 0.0), axis=0)]
    unnamed x370 -> x56, local copies, waits for them, and re-layouts: 34.2 us -> 9.02 us
    psum x1 -> x0, blocking collectives: 22.2 us -> none  [per_device(): lax.psum((grad_mask_embed, grad_self_qkv, grad_self_out, grad_cross_qkv,...]
  transfers between devices with their start and end apart: 9 -> 0, of which waited for: 9 -> 0; matrix products, arithmetic and copies ran while one was open for 4% -> 0% of each run, Pallas kernels for 0% -> 0%
where the time goes in v1:
time: 455 us; the launch traced here: 452 us
  Pallas kernels  409 us (90%)
  local copies, waits for them, and re-layouts  26.3 us (6%)
  other arithmetic  15.9 us (3%)
    pallas_call x1, Pallas kernels, gather_weights(): pl.pallas_call(functools.partial(gather_kernel, tn_, groups), in_specs=[p...  145 us
    pallas_call x1, Pallas kernels, sum_over_plane(): pl.pallas_call(functools.partial(sum_kernel, count), in_specs=[pl.BlockSp...  77.6 us
    pallas_call x3, Pallas kernels, call_attend_bwd(): pl.pallas_call(functools.partial(attend_bwd, cross), grid=(4,), in_specs=...  66.6 us
    pallas_call x3, Pallas kernels, call_attend_fwd(): pl.pallas_call(functools.partial(attend_fwd, cross, from_norm), grid=(4,)...  62.5 us
    pallas_call x2, Pallas kernels, call_ffn_fwd(): pl.pallas_call(ffn_fwd, grid=(4,), in_specs=[rows_of(512), whole((1, 512)...  28.7 us
    pallas_call x2, Pallas kernels, call_ffn_bwd(): pl.pallas_call(functools.partial(ffn_bwd, len(dys) == 2), grid=(4,), in_s...  28 us

profile of v1, /device:TPU:17, one launch (start us, length us, event | category | flops | bytes accessed | tf_op | source)
XLA Modules:
  0.0 452.1 jit_solution(18046488427103969136)
XLA Ops:
  4.6 1.6 fusion.6
  6.3 1.2 copy.56
  8.9 1.2 copy.58
  16.3 1.0 copy.61.refs_6_
  18.3 1.1 pad_maximum_fusion.1.refs_4_.refs_5_
  19.4 1.0 pad_maximum_fusion.refs_4_.refs_6_
  20.5 1.3 fusion.5.refs_4_.refs_12_.refs_13_
  21.8 1.6 convert_select_fusion.refs_1_
  23.4 145.5 %shard_map.323 = (f32[3,2,4,64,512]{4,3,2,1,0:T(8,128)}, f32[3,2,4,128,512]{4,3,2,1,0:T(8,128)}, f32[3,2,4,64,512]{4,3,2,1,0:T(8,128)}, f32[3,2,4,64,512]{4,3,2,1,0:T(8,128)}, f32[3,2,4,128,512]{4,3,2,1,0:T(8,128)}) custom-call(f32[64,512]{1,0:T(8,128)} %bitcast_convert_fusion.4.refs_0_, f32[128,512]{1,0:T(8,128)} %bitcast_convert_fusion.1.refs_1_, ...), custom_call_target="tpu_custom_call" | custom-call | tf_op jit(solution)/shard_map/pallas_call | solution.py:505
  168.9 20.8 %shard_map.326 = (f32[1024,512]{1,0:T(8,128)}, f32[1024,1]{1,0:T(8,128)}, bf16[1024,512]{1,0:T(8,128)(2,1)}, bf16[4,4,512,512]{3,2,1,0:T(8,128)(2,1)}, bf16[1024...) custom-call(s32[8]{0:T(128)} %pad_add_fusion.refs_0_, ...), custom_call_target="tpu_custom_call" | custom-call | tf_op jit(solution)/shard_map/pallas_call | solution.py:282
  189.7 20.1 %shard_map.324 = (f32[1024,512]{1,0:T(8,128)}, f32[1024,1]{1,0:T(8,128)}, bf16[1024,512]{1,0:T(8,128)(2,1)}, bf16[4,4,512,512]{3,2,1,0:T(8,128)(2,1)}, bf16[1024...) custom-call(s32[8]{0:T(128)} %pad_add_fusion.refs_0_, ...), custom_call_target="tpu_custom_call" | custom-call | tf_op jit(solution)/shard_map/pallas_call | solution.py:282
  209.8 14.3 %shard_map.325 = (f32[1024,512]{1,0:T(8,128)}, f32[1024,1]{1,0:T(8,128)}, bf16[1024,512]{1,0:T(8,128)(2,1)}, bf16[1024,512]{1,0:T(8,128)(2,1)}, bf16[1024,2048]{1,0:T(8,128)(2,1)}) custom-call(f32[1024,512]{1,0:T(8,128)} %get-tuple-element.89.refs_0_.refs_2_, f32[1,512]{1,0:T(1,128)} %get-tuple-element.180.refs_2_.refs_9_.refs_1_.refs_4_, ...), custom_call_target="tpu_custom_call" | custom-call | tf_op jit(solution)/shard_map/pallas_call | solution.py:355
  224.2 21.6 %shard_map.327 = (f32[1024,512]{1,0:T(8,128)}, f32[1024,1]{1,0:T(8,128)}, bf16[1024,512]{1,0:T(8,128)(2,1)}, bf16[4,4,1024,512]{3,2,1,0:T(8,128)(2,1)}, bf16[102...) custom-call(s32[8]{0:T(128)} %pad_add_fusion.refs_0_, ...), custom_call_target="tpu_custom_call" | custom-call | tf_op jit(solution)/shard_map/pallas_call | solution.py:282
  245.7 14.3 %shard_map.328 = (f32[1024,512]{1,0:T(8,128)}, f32[1024,1]{1,0:T(8,128)}, bf16[1024,512]{1,0:T(8,128)(2,1)}, bf16[1024,512]{1,0:T(8,128)(2,1)}, bf16[1024,2048]{1,0:T(8,128)(2,1)}) custom-call(f32[1024,512]{1,0:T(8,128)} %get-tuple-element.96.refs_0_.refs_2_, f32[1,512]{1,0:T(1,128)} %get-tuple-element.179.refs_9_.refs_1_.refs_4_, ...), custom_call_target="tpu_custom_call" | custom-call | tf_op jit(solution)/shard_map/pallas_call | solution.py:355
  260.1 13.9 %shard_map.329 = (f32[1024,512]{1,0:T(8,128)}, f32[512,512]{1,0:T(8,128)}, f32[512,512]{1,0:T(8,128)}, f32[8,512]{1,0:T(8,128)}) custom-call(bf16[1024,512]{1,0:T(8,128)(2,1)} %bitcast.123, f32[1024,512]{1,0:T(8,128)} %get-tuple-element.100.refs_1_, f32[1024,1]{1,0:T(8,128)} %get-tuple-element.101.refs_2_, f32[1,512]{1,0:T(1,128)} %get-tuple-element.183.refs_6_.refs_3_, ...), custom_call_target="tpu_custom_call" | custom-call | tf_op jit(solution)/shard_map/pallas_call | solution.py:382
  274.0 23.2 %shard_map.330 = (f32[1024,512]{1,0:T(8,128)}, f32[1024,512]{1,0:T(8,128)}, f32[3,128,512]{2,1,0:T(8,128)}, f32[128,512]{1,0:T(8,128)}, f32[8,512]{1,0:T(8,128)}) custom-call(s32[8]{0:T(128)} %pad_add_fusion.refs_0_, f32[1024,512]{1,0:T(8,128)} %get-tuple-element.104.refs_1_, f32[1024,512]{1,0:T(8,128)} %get-tuple-element.96.refs_0_.refs_2_, ...), custom_call_target="tpu_custom_call" | custom-call | tf_op jit(solution)/shard_map/pallas_call | solution.py:327
  297.2 21.8 %shard_map.333 = (f32[1024,512]{1,0:T(8,128)}, f32[3,128,512]{2,1,0:T(8,128)}, f32[128,512]{1,0:T(8,128)}, f32[8,512]{1,0:T(8,128)}) custom-call(s32[8]{0:T(128)} %pad_add_fusion.refs_0_, f32[1024,512]{1,0:T(8,128)} %get-tuple-element.125.refs_1_, f32[1024,512]{1,0:T(8,128)} %get-tuple-element.94.refs_1_.refs_2_, f32[1024,1]{1,0:T(8,128)} %get-tuple-element.126.refs_3_, ...), custom_call_target="tpu_custom_call" | custom-call | tf_op jit(solution)/shard_map/pallas_call | solution.py:327
  319.1 14.1 %shard_map.331 = (f32[1024,512]{1,0:T(8,128)}, f32[512,512]{1,0:T(8,128)}, f32[512,512]{1,0:T(8,128)}, f32[8,512]{1,0:T(8,128)}) custom-call(bf16[1024,512]{1,0:T(8,128)(2,1)} %bitcast.124, f32[1024,512]{1,0:T(8,128)} %get-tuple-element.112.refs_1_, f32[1024,512]{1,0:T(8,128)} %get-tuple-element.113.refs_2_, f32[1024,1]{1,0:T(8,128)} %get-tuple-element.114.refs_3_, ...), custom_call_target="tpu_custom_call" | custom-call | tf_op jit(solution)/shard_map/pallas_call | solution.py:382
  333.2 21.5 %shard_map.332 = (f32[1024,512]{1,0:T(8,128)}, f32[3,128,512]{2,1,0:T(8,128)}, f32[128,512]{1,0:T(8,128)}, f32[8,512]{1,0:T(8,128)}) custom-call(s32[8]{0:T(128)} %pad_add_fusion.refs_0_, f32[1024,512]{1,0:T(8,128)} %get-tuple-element.117.refs_1_, f32[1024,512]{1,0:T(8,128)} %get-tuple-element.89.refs_0_.refs_2_, f32[1024,1]{1,0:T(8,128)} %get-tuple-element.118.refs_3_, ...), custom_call_target="tpu_custom_call" | custom-call | tf_op jit(solution)/shard_map/pallas_call | solution.py:327
  354.7 1.6 select_reduce_fusion
  360.9 77.6 %shard_map.334 = (f32[2,2,2,48,512]{4,3,2,1,0:T(8,128)}, f32[2,2,2,16,512]{4,3,2,1,0:T(8,128)}, f32[2,2,2,64,512]{4,3,2,1,0:T(8,128)}, f32[2,2,2,64,512]{4,3,2,1...) custom-call(f32[2,2,2,48,512]{4,3,2,1,0:T(8,128)} %bitcast.135, ...), custom_call_target="tpu_custom_call" | custom-call | tf_op jit(solution)/shard_map/pallas_call | solution.py:611
  439.5 2.3 copy.64
  443.6 1.1 copy.65
  444.8 1.1 copy.66
  (84 shorter events, 25.8 us)
Async XLA Ops:
  0.7 9.6 %copy-start.13 = (bf16[128,512]{1,0:T(8,128)(2,1)S(1)}, bf16[128,512]{1,0:T(8,128)(2,1)}, u32[]{:S(2)}) copy-start(bf16[128,512]{1,0:T(8,128)(2,1)} %param.33) | copy-start | bytes 393220
  0.7 9.6 %copy-start.14 = (bf16[128,512]{1,0:T(8,128)(2,1)S(1)}, bf16[128,512]{1,0:T(8,128)(2,1)}, u32[]{:S(2)}) copy-start(bf16[128,512]{1,0:T(8,128)(2,1)} %param.31) | copy-start | bytes 393220
  0.7 9.4 %copy-start.15 = (bf16[3,512,128]{2,1,0:T(8,128)(2,1)S(1)}, bf16[3,512,128]{2,1,0:T(8,128)(2,1)}, u32[]{:S(2)}) copy-start(bf16[3,512,128]{2,1,0:T(8,128)(2,1)} %param.32) | copy-start | bytes 1179652
  10.0 3.4 copy-start.12
  10.3 4.0 copy-start.10
  11.6 2.8 copy-start.11
  12.5 2.3 copy-start.2
  12.5 2.3 copy-start.3
  14.5 1.8 copy-start.20
  14.7 2.6 copy-start.19
  18.3 2.2 copy-start
  18.3 2.2 copy-start.21
  333.2 21.5 %copy-start.1 = (f32[1024,512]{1,0:T(8,128)S(1)}, f32[1024,512]{1,0:T(8,128)}, u32[]{:S(2)}) copy-start(f32[1024,512]{1,0:T(8,128)} %get-tuple-element.132) | copy-start | bytes 6291460
  438.5 5.1 %copy-start.9 = (f32[2,2,2,48,512]{4,3,2,1,0:T(8,128)S(1)}, f32[2,2,2,48,512]{4,3,2,1,0:T(8,128)}, u32[]{:S(2)}) copy-start(f32[2,2,2,48,512]{4,3,2,1,0:T(8,128)} %get-tuple-element.153) | copy-start | bytes 2359300
  438.5 6.3 %copy-start.8 = (f32[2,2,2,48,512]{4,3,2,1,0:T(8,128)S(1)}, f32[2,2,2,48,512]{4,3,2,1,0:T(8,128)}, u32[]{:S(2)}) copy-start(f32[2,2,2,48,512]{4,3,2,1,0:T(8,128)} %get-tuple-element.155) | copy-start | bytes 2359300
  439.5 6.5 %copy-start.18 = (f32[2,2,2,16,512]{4,3,2,1,0:T(8,128)S(1)}, f32[2,2,2,16,512]{4,3,2,1,0:T(8,128)}, u32[]{:S(2)}) copy-start(f32[2,2,2,16,512]{4,3,2,1,0:T(8,128)} %get-tuple-element.150) | copy-start | bytes 786436
  441.8 4.8 %copy-start.7 = (f32[2,2,2,64,512]{4,3,2,1,0:T(8,128)S(1)}, f32[2,2,2,64,512]{4,3,2,1,0:T(8,128)}, u32[]{:S(2)}) copy-start(f32[2,2,2,64,512]{4,3,2,1,0:T(8,128)} %get-tuple-element.151) | copy-start | bytes 3145732
  444.8 2.8 copy-start.6
  446.6 2.0 copy-start.17
  446.6 2.7 copy-start.16
  447.6 2.4 copy-start.5
  448.6 2.4 copy-start.4
